TPU v7x, 128 devices: a whole 4x4x4 slice. The times are simulated.
128 devices in a mesh: dp: 4 (over y), context: 16 (over x, z), head: 2 (over core).
Axes of the slice: x: 4, y: 4, z: 4, core: 2. Of those that a mesh axis runs over, the one named last changes fastest.
Arguments:
- long_q: bfloat16 [4, 1024, 4096], P('dp', 'context', 'head'), may hold values from -5 to 5
- long_k: bfloat16 [4, 1024, 512], P('dp', 'context', 'head'), may hold values from -5 to 5
- long_v: bfloat16 [4, 1024, 512], P('dp', 'context', 'head'), may hold values from -6 to 6
- long_dout: bfloat16 [4, 1024, 4096], P('dp', 'context', 'head'), may hold values from -6 to 6
- short_q: bfloat16 [4, 2048, 4096], P('dp', 'context', 'head'), may hold values from -5 to 5
- short_k: bfloat16 [4, 2048, 512], P('dp', 'context', 'head'), may hold values from -5 to 5
- short_v: bfloat16 [4, 2048, 512], P('dp', 'context', 'head'), may hold values from -6 to 6
- short_dout: bfloat16 [4, 2048, 4096], P('dp', 'context', 'head'), may hold values from -6 to 6
- short_lengths: int32 [4, 16, 7], P('dp', 'context'), may hold values from 1 to 32, as said below
Outputs:
- long_dq: bfloat16 [4, 1024, 4096], P('dp', 'context', 'head')
- long_dk: bfloat16 [4, 1024, 512], P('dp', 'context', 'head')
- long_dv: bfloat16 [4, 1024, 512], P('dp', 'context', 'head')
- short_dq: bfloat16 [4, 2048, 4096], P('dp', 'context', 'head')
- short_dk: bfloat16 [4, 2048, 512], P('dp', 'context', 'head')
- short_dv: bfloat16 [4, 2048, 512], P('dp', 'context', 'head')
Inputs may be any that keep to these rules, and one draw needn't show every extreme that they name: `short_lengths`: every block of 128 short tokens holds 7 documents whose lengths sum to 128: the first is 32 long, and the second and third, the fourth and fifth, the sixth and seventh each sum to 32.
All inputs are finite; a program needn't handle non-finite values.
Results may differ from a plain program's by a relative error of at most 0.018.
Values may be sent and summed in bfloat16 or wider, within the bound.
A program may use at most 64 MiB of HBM per device.

v0:
```python
import functools
import math

import jax
import jax.numpy as jnp
from jax import lax
from jax.experimental import pallas as pl
from jax.experimental.pallas import tpu as pltpu
from jax.sharding import PartitionSpec as P

HEAD = 128
KV = 2
GROUP = 8
LONG = 64
SHORT = 128
SEG = 32
DOCS = 7
N = 16
PER = 4
CHUNK = PER * LONG
ROWS = GROUP * LONG
QW = GROUP * HEAD
MESH = pl.DeviceIdType.MESH
SCALE = 1.0 / math.sqrt(HEAD)
SCALE2 = SCALE * math.log2(math.e)
NEG = -1e30
NT = (((1,), (1,)), ((), ()))
TN = (((0,), (0,)), ((), ()))


def nt(a, b):
    return lax.dot_general(a, b, NT, preferred_element_type=jnp.float32)


def tn(a, b):
    return lax.dot_general(a, b, TN, preferred_element_type=jnp.float32)


def nn(a, b):
    return jnp.dot(a, b, preferred_element_type=jnp.float32)


def kernel(
    lq,
    lk,
    lv,
    ldo,
    sq,
    sk,
    sv,
    sdo,
    lens_hbm,
    dq_o,
    dk_o,
    dv_o,
    sdq_o,
    sdk_o,
    sdv_o,
    sq_in,
    sk_in,
    sv_in,
    sdo_in,
    q_in,
    do_in,
    q_s,
    do_s,
    k_all,
    v_all,
    e_s,
    gp_s,
    gs_s,
    w_s,
    d_s,
    acc_s,
    dv_out,
    dk_out,
    dv_in,
    dk_in,
    dq_out,
    dq_in,
    lens,
    in_sem,
    k_send_x,
    k_send_z,
    k_recv,
    v_send_x,
    v_send_z,
    v_recv,
    dv_send,
    dv_recv,
    dk_send,
    dk_recv,
    q_sem,
    do_sem,
    dq_sem,
):
    me = lax.axis_index("context")
    dp = lax.axis_index("dp")
    hd = lax.axis_index("head")
    x = me // PER
    z = me % PER
    crossed = hd == 0

    def partner_of(r):
        return jnp.where(crossed, PER - 1 - r, r + 1 - 2 * (r % 2))

    def head_of(r):
        return (r > partner_of(r)).astype(jnp.int32)

    def last_of(r):
        return jnp.maximum(r, partner_of(r))

    mine = head_of(x)
    other = 1 - mine
    high = last_of(x)
    low = jnp.minimum(x, partner_of(x))
    partner = partner_of(x) * PER + z
    kv_mine = pl.ds(pl.multiple_of(mine * HEAD, HEAD), HEAD)
    q_mine = pl.ds(pl.multiple_of(mine * QW, QW), QW)
    q_other = pl.ds(pl.multiple_of(other * QW, QW), QW)

    def dev(j):
        return (dp, j, hd)

    barrier = pltpu.get_barrier_semaphore()
    for d in range(1, N):
        pl.semaphore_signal(
            barrier, inc=1, device_id=dev(lax.rem(me + d, N)), device_id_type=MESH
        )

    loads = [
        pltpu.make_async_copy(src, dst, in_sem.at[i])
        for i, (src, dst) in enumerate(
            (
                (lk.at[:, kv_mine], k_all.at[me]),
                (lv.at[:, kv_mine], v_all.at[me]),
                (sq, sq_in),
                (sk, sk_in),
                (sdo, sdo_in),
                (sv, sv_in),
                (lens_hbm, lens),
                (lq.at[:, q_mine], q_in.at[mine]),
                (ldo.at[:, q_mine], do_in.at[mine]),
            )
        )
    ]
    for load in loads:
        load.start()
    for b in range(PER):

        @pl.when(b > z)
        def _():
            k_all[high * PER + b] = jnp.zeros((LONG, HEAD), jnp.bfloat16)
            v_all[high * PER + b] = jnp.zeros((LONG, HEAD), jnp.bfloat16)

    pl.semaphore_wait(barrier, N - 1)

    def copy(src, dst, send, recv, j):
        return pltpu.make_async_remote_copy(src, dst, send, recv, dev(j), MESH)

    def along_x(src, dst, send, recv):
        for r in range(PER):
            h = pl.ds(pl.multiple_of(head_of(r) * HEAD, HEAD), HEAD)
            yield (
                (x != r) & (x <= last_of(r)),
                copy(src.at[:, h], dst.at[me], send.at[r], recv.at[me], r * PER + z),
            )

    def along_z(src, dst, send, recv, b):
        for d in range(PER):
            yield (
                (z != d) & ((b < high) | ((b == high) & (d > z))),
                copy(
                    src,
                    dst.at[b * PER + z],
                    send.at[b * PER + d],
                    recv.at[b * PER + z],
                    x * PER + d,
                ),
            )

    def to_all(src, dst, send, recv):
        for r in (3, 2, 1, 0):
            h = pl.ds(pl.multiple_of(head_of(r) * HEAD, HEAD), HEAD)
            for d in range(PER):
                j = r * PER + d
                yield (
                    (me != j) & ((x < last_of(r)) | ((x == last_of(r)) & (z <= d))),
                    copy(src.at[:, h], dst.at[me], send.at[j], recv.at[me], j),
                )

    def wait_direct(dst, recv, b):
        for d in range(PER):
            j = b * PER + d

            @pl.when((me != j) & ((b < high) | ((b == high) & (d <= z))))
            def _():
                copy(dst.at[me], dst.at[j], recv.at[j], recv.at[j], me).wait_recv()

    def each(copies, act):
        for on, c in copies:

            @pl.when(on)
            def _():
                act(c)

    def start(c):
        c.start()

    def forward(dst, send_z, recv):
        for b in range(PER):

            @pl.when((x != b) & (b <= high))
            def _():
                copy(
                    dst.at[me], dst.at[b * PER + z], send_z.at[0], recv.at[b * PER + z], me
                ).wait_recv()
                each(along_z(dst.at[b * PER + z], dst, send_z, recv, b), start)

    def wait_row(dst, recv, b):
        for d in range(PER):

            @pl.when((z != d) & ((b < high) | ((b == high) & (d < z))))
            def _():
                copy(
                    dst.at[me], dst.at[b * PER + d], recv.at[b * PER + d], recv.at[b * PER + d], me
                ).wait_recv()

    def q_copy(src, dst, sem):
        return copy(src.at[:, q_other], dst.at[mine], sem.at[0], sem.at[1], partner)

    each(along_x(lv, v_all, v_send_x, v_recv), start)
    each(to_all(lk, k_all, k_send_z, k_recv), start)
    each(along_z(lv.at[:, kv_mine], v_all, v_send_z, v_recv, x), start)
    q_copy(lq, q_in, q_sem).start()
    q_copy(ldo, do_in, do_sem).start()

    for i in (0, 1):
        loads[i].wait()
    forward(v_all, v_send_z, v_recv)

    def spread(src, dst, p):
        for g in range(GROUP):
            dst[p, g * LONG : (g + 1) * LONG] = src[p, :, g * HEAD : (g + 1) * HEAD]

    offset = lax.broadcasted_iota(jnp.int32, (CHUNK, ROWS), 0) - lax.rem(
        lax.broadcasted_iota(jnp.int32, (CHUNK, ROWS), 1), LONG
    )
    def by_count(p, act):
        for n in range(1 + p, PER + p):

            @pl.when((low, high)[p] == n - 1)
            def _():
                act(p, n)

    def by_pair(act):
        for few, many in ((1, 4), (2, 3), (1, 2), (3, 4)):

            @pl.when((low == few - 1) & (high == many - 1))
            def _():
                act(few, many)

    def keys_of(ref, c, n=1):
        return ref[c * PER : (c + n) * PER].reshape(n * CHUNK, HEAD)

    def scores(p, n):
        tops = []
        sums = []
        for c in range(n):
            s = nt(keys_of(k_all, c), q_s[p])
            if c == n - 1:
                s = jnp.where(offset <= z * LONG, s, NEG)
            m = jnp.max(s, axis=0, keepdims=True)
            e = jnp.exp2((s - m) * SCALE2)
            e_s[p, c] = e
            tops.append(m)
            sums.append(jnp.sum(e, axis=0, keepdims=True))
        top = tops[0]
        for m in tops[1:]:
            top = jnp.maximum(top, m)
        factors = [jnp.exp2((m - top) * SCALE2) for m in tops]
        total = factors[0] * sums[0]
        for c in range(1, n):
            total = total + factors[c] * sums[c]
        inverse = 1.0 / total
        for c in range(n):
            w_s[p, c] = factors[c] * inverse

    def grad_copy(src, dst, send, recv, b, d):
        j = b * PER + d
        return copy(src.at[j], dst.at[me], send.at[j], recv.at[me], j)

    def is_sent(b, d):
        return (me != b * PER + d) & ((b < high) | ((b == high) & (d <= z)))

    def send_chunk(total, src, dst, send, recv, b):
        part = total.astype(jnp.bfloat16).reshape(PER, LONG, HEAD)
        src[pl.ds(b * PER, PER)] = part
        for d in range(PER):

            @pl.when(is_sent(b, d))
            def _():
                grad_copy(src, dst, send, recv, b, d).start()

    def shares(product, dst, few, many):
        for c in range(many):
            total = product(1, c)
            if c < few:
                total = total + product(0, c)
            send_chunk(total, *dst, c)

    def value_product(p, c):
        return nn((e_s[p, c] * w_s[p, c]).astype(jnp.bfloat16), do_s[p])

    def key_product(p, c):
        gs = (e_s[p, c] * (w_s[p, c] * (gp_s[p, c] - d_s[p]))).astype(jnp.bfloat16)
        gs_s[p, c] = gs
        return nn(gs, q_s[p]) * SCALE

    def prob_grads(p, n):
        delta = jnp.zeros((1, ROWS), jnp.float32)
        for c in range(n):
            gp = nt(keys_of(v_all, c), do_s[p])
            gp_s[p, c] = gp
            delta = delta + w_s[p, c] * jnp.sum(e_s[p, c] * gp, axis=0, keepdims=True)
        d_s[p] = delta

    def query_grads(p, n):
        gs = gs_s[p, :n].reshape(n * CHUNK, ROWS)
        return (tn(gs, keys_of(k_all, 0, n)) * SCALE).astype(jnp.bfloat16)

    dv_ends = (dv_out, dv_in, dv_send, dv_recv)
    dk_ends = (dk_out, dk_in, dk_send, dk_recv)
    loads[7].wait()
    spread(q_in, q_s, mine)
    q_copy(lq, q_in, q_sem).wait_recv()
    spread(q_in, q_s, other)
    for b in range(PER):
        wait_direct(k_all, k_recv, b)

    def both_scores(few, many):
        scores(0, few)
        scores(1, many)

    by_pair(both_scores)
    loads[8].wait()
    spread(do_in, do_s, mine)
    q_copy(ldo, do_in, do_sem).wait_recv()
    spread(do_in, do_s, other)
    by_pair(functools.partial(shares, value_product, dv_ends))
    for b in range(PER):
        wait_row(v_all, v_recv, b)

    def both_key_grads(few, many):
        prob_grads(0, few)
        prob_grads(1, many)
        shares(key_product, dk_ends, few, many)

    by_pair(both_key_grads)

    def store_query_grads(p, n):
        grad = query_grads(p, n)
        for g in range(GROUP):
            dq_out[p, :, g * HEAD : (g + 1) * HEAD] = grad[g * LONG : (g + 1) * LONG]

    dq_copy = copy(dq_out.at[other], dq_in, dq_sem.at[0], dq_sem.at[1], partner)
    for p in range(KV):
        by_count(p, store_query_grads)
        pl.when(other == p)(dq_copy.start)
    for h in range(KV):

        @pl.when(mine == h)
        def _():
            dq_o[:, h * QW : (h + 1) * QW] = dq_out[mine]

    for i in (2, 3, 4, 5, 6):
        loads[i].wait()
    ends = []
    total = jnp.int32(0)
    for i in range(DOCS):
        total = total + lens[0, 0, i]
        ends.append(total)
    outs = []
    for seg in range(SHORT // SEG):
        base = seg * SEG
        key_pos = base + lax.broadcasted_iota(jnp.int32, (SEG, GROUP * SEG), 0)
        query_pos = base + lax.rem(
            lax.broadcasted_iota(jnp.int32, (SEG, GROUP * SEG), 1), SEG
        )
        key_doc = jnp.zeros((SEG, GROUP * SEG), jnp.int32)
        query_doc = jnp.zeros((SEG, GROUP * SEG), jnp.int32)
        for end in ends:
            key_doc = key_doc + (key_pos >= end).astype(jnp.int32)
            query_doc = query_doc + (query_pos >= end).astype(jnp.int32)
        allowed = (key_doc == query_doc) & (key_pos <= query_pos)
        rows = slice(base, base + SEG)
        for h in range(KV):
            kv = slice(h * HEAD, (h + 1) * HEAD)
            cols = [
                slice((h * GROUP + g) * HEAD, (h * GROUP + g + 1) * HEAD)
                for g in range(GROUP)
            ]
            q = jnp.concatenate([sq_in[rows, c] for c in cols], axis=0)
            do = jnp.concatenate([sdo_in[rows, c] for c in cols], axis=0)
            k = sk_in[rows, kv]
            v = sv_in[rows, kv]
            s = jnp.where(allowed, nt(k, q), NEG)
            e = jnp.exp2((s - jnp.max(s, axis=0, keepdims=True)) * SCALE2)
            p = e * (1.0 / jnp.sum(e, axis=0, keepdims=True))
            gp = nt(v, do)
            delta = jnp.sum(p * gp, axis=0, keepdims=True)
            gs = (p * (gp - delta)).astype(jnp.bfloat16)
            sdv_o[rows, kv] = nn(p.astype(jnp.bfloat16), do).astype(jnp.bfloat16)
            sdk_o[rows, kv] = (nn(gs, q) * SCALE).astype(jnp.bfloat16)
            dq = (tn(gs, k) * SCALE).astype(jnp.bfloat16)
            for g, c in enumerate(cols):
                sdq_o[rows, c] = dq[g * SEG : (g + 1) * SEG]

    def wait_send(c):
        c.wait_send()

    each(to_all(lk, k_all, k_send_z, k_recv), wait_send)
    each(along_x(lv, v_all, v_send_x, v_recv), wait_send)
    for b in range(PER):
        each(along_z(v_all.at[b * PER + z], v_all, v_send_z, v_recv, b), wait_send)
        for d in range(PER):

            @pl.when(is_sent(b, d))
            def _():
                grad_copy(dv_out, dv_in, dv_send, dv_recv, b, d).wait_send()
                grad_copy(dk_out, dk_in, dk_send, dk_recv, b, d).wait_send()

    q_copy(lq, q_in, q_sem).wait_send()
    q_copy(ldo, do_in, do_sem).wait_send()
    dq_copy.wait_send()

    def sums(src, dst, recv, out):
        for h in range(KV):
            kv = slice(h * HEAD, (h + 1) * HEAD)

            @pl.when(mine == h)
            def _():
                acc_s[0] = src[me].astype(jnp.float32)

            @pl.when(mine != h)
            def _():
                acc_s[0] = jnp.zeros((LONG, HEAD), jnp.float32)

            for i in range(2):
                r = jnp.where(crossed, 2 * h + i, 2 * i + h)
                last = last_of(r)
                for d in range(PER):
                    j = r * PER + d

                    @pl.when((me != j) & ((x < last) | ((x == last) & (z <= d))))
                    def _():
                        copy(src.at[me], dst.at[j], recv.at[j], recv.at[j], me).wait_recv()
                        acc_s[0] += dst[j].astype(jnp.float32)

            out[:, kv] = acc_s[0].astype(jnp.bfloat16)

    sums(dv_out, dv_in, dv_recv, dv_o)
    sums(dk_out, dk_in, dk_recv, dk_o)
    dq_copy.wait_recv()
    for h in range(KV):

        @pl.when(mine != h)
        def _():
            dq_o[:, h * QW : (h + 1) * QW] = dq_in[...]


def write_results(*refs):
    sem = refs[12]
    copies = [pltpu.make_async_copy(refs[i], refs[6 + i], sem.at[i]) for i in range(6)]
    for copy in copies:
        copy.start()
    for copy in copies:
        copy.wait()


def on_device(lq, lk, lv, ldo, sq, sk, sv, sdo, lens):
    bf, f32 = jnp.bfloat16, jnp.float32
    args = (lq[0], lk[0], lv[0], ldo[0], sq[0], sk[0], sv[0], sdo[0], lens)
    kv, qw = KV * HEAD, KV * GROUP * HEAD
    shapes = [(LONG, qw), (LONG, kv), (LONG, kv), (SHORT, qw), (SHORT, kv), (SHORT, kv)]
    any_spec = pl.BlockSpec(memory_space=pltpu.HBM)
    vmem_spec = pl.BlockSpec(memory_space=pltpu.VMEM)
    outs = pl.pallas_call(
        kernel,
        out_shape=[pltpu.VMEM(s, bf) for s in shapes],
        in_specs=[any_spec] * 9,
        out_specs=[vmem_spec] * 6,
        scratch_shapes=[
            pltpu.VMEM((SHORT, qw), bf),
            pltpu.VMEM((SHORT, kv), bf),
            pltpu.VMEM((SHORT, kv), bf),
            pltpu.VMEM((SHORT, qw), bf),
            pltpu.VMEM((KV, LONG, QW), bf),
            pltpu.VMEM((KV, LONG, QW), bf),
            pltpu.VMEM((KV, ROWS, HEAD), bf),
            pltpu.VMEM((KV, ROWS, HEAD), bf),
            pltpu.VMEM((N, LONG, HEAD), bf),
            pltpu.VMEM((N, LONG, HEAD), bf),
            pltpu.VMEM((KV, PER, CHUNK, ROWS), f32),
            pltpu.VMEM((KV, PER, CHUNK, ROWS), f32),
            pltpu.VMEM((KV, PER, CHUNK, ROWS), bf),
            pltpu.VMEM((KV, PER, 1, ROWS), f32),
            pltpu.VMEM((KV, 1, ROWS), f32),
            pltpu.VMEM((1, LONG, HEAD), f32),
            pltpu.VMEM((N, LONG, HEAD), bf),
            pltpu.VMEM((N, LONG, HEAD), bf),
            pltpu.VMEM((N, LONG, HEAD), bf),
            pltpu.VMEM((N, LONG, HEAD), bf),
            pltpu.VMEM((KV, LONG, QW), bf),
            pltpu.VMEM((LONG, QW), bf),
            pltpu.SMEM((1, 1, DOCS), jnp.int32),
            pltpu.SemaphoreType.DMA((9,)),
        ]
        + [pltpu.SemaphoreType.DMA((n,)) for n in (PER, N, N) * 2 + (N,) * 4 + (2,) * 3],
        compiler_params=pltpu.CompilerParams(
            collective_id=0, has_side_effects=True, vmem_limit_bytes=40 << 20
        ),
        name="attention_grads",
    )(*(pltpu.with_memory_space_constraint(a, pltpu.HBM) for a in args))
    outs = pl.pallas_call(
        write_results,
        out_shape=[jax.ShapeDtypeStruct(s, bf) for s in shapes],
        in_specs=[vmem_spec] * 6,
        out_specs=[any_spec] * 6,
        scratch_shapes=[pltpu.SemaphoreType.DMA((6,))],
        compiler_params=pltpu.CompilerParams(vmem_limit_bytes=1 << 20),
        name="write_results",
    )(*(pltpu.with_memory_space_constraint(o, pltpu.VMEM) for o in outs))
    return tuple(o[None] for o in outs)


def solution(mesh):
    spec = P("dp", "context", "head")
    return jax.shard_map(
        on_device,
        mesh=mesh,
        in_specs=(spec,) * 8 + (P("dp", "context", None),),
        out_specs=(spec,) * 6,
        check_vma=False,
    )
```

profile of v0, /device:TPU:1, one launch (start us, length us, event | category | flops | bytes accessed | tf_op | source)
XLA Modules:
  0.0 26.3 jit_solution(9171882045315020728)
XLA Ops:
  0.6 24.5 %attention_grads.1 = (bf16[64,2048]{1,0:T(8,128)(2,1)S(1)}, bf16[64,256]{1,0:T(8,128)(2,1)S(1)}, bf16[64,256]{1,0:T(8,128)(2,1)S(1)}, bf16[128,2048]{1,0:T(8,128...) custom-call(bf16[64,2048]{1,0:T(8,128)(2,1)} %bitcast.16, bf16[64,256]{1,0:T(8,128)(2,1)} %bitcast.20, ...), custom_call_target="tpu_custom_call" | custom-call | tf_op jit(solution)/shard_map/attention_grads/pallas_call | solution.py:488
  25.1 1.0 %write_results.1 = (bf16[64,2048]{1,0:T(8,128)(2,1)}, bf16[64,256]{1,0:T(8,128)(2,1)}, bf16[64,256]{1,0:T(8,128)(2,1)}, bf16[128,2048]{1,0:T(8,128)(2,1)}, bf16[...) custom-call(bf16[64,2048]{1,0:T(8,128)(2,1)S(1)} %get-tuple-element.18.refs_0_, ...), custom_call_target="tpu_custom_call" | custom-call | tf_op jit(solution)/shard_map/write_results/pallas_call | solution.py:525
where the time goes:
time: 26.4 us; the launch traced here: 26.3 us
  Pallas kernels  25.5 us (97%)
  between operations  0.8 us (3%)
    pallas_call x1, Pallas kernels, on_device(): pl.pallas_call(kernel, out_shape=[pltpu.VMEM(s, bf) for s in shapes], in_...  24.5 us
    pallas_call x1, Pallas kernels, on_device(): pl.pallas_call(write_results, out_shape=[jax.ShapeDtypeStruct(s, bf) for...  0.99 us

commit v1 on v0

--- a/solution.py
+++ b/solution.py
@@ -231,9 +231,9 @@
 
     each(along_x(lv, v_all, v_send_x, v_recv), start)
     each(to_all(lk, k_all, k_send_z, k_recv), start)
-    each(along_z(lv.at[:, kv_mine], v_all, v_send_z, v_recv, x), start)
     q_copy(lq, q_in, q_sem).start()
     q_copy(ldo, do_in, do_sem).start()
+    each(along_z(lv.at[:, kv_mine], v_all, v_send_z, v_recv, x), start)
 
     for i in (0, 1):
         loads[i].wait()
@@ -333,6 +333,8 @@
     dk_ends = (dk_out, dk_in, dk_send, dk_recv)
     loads[7].wait()
     spread(q_in, q_s, mine)
+    loads[8].wait()
+    spread(do_in, do_s, mine)
     q_copy(lq, q_in, q_sem).wait_recv()
     spread(q_in, q_s, other)
     for b in range(PER):
@@ -343,8 +345,6 @@
         scores(1, many)
 
     by_pair(both_scores)
-    loads[8].wait()
-    spread(do_in, do_s, mine)
     q_copy(ldo, do_in, do_sem).wait_recv()
     spread(do_in, do_s, other)
     by_pair(functools.partial(shares, value_product, dv_ends))

time: 26.4 us -> 26.4 us (level)
  no operation moved by 1% of the time
where the time goes in v1:
time: 26.4 us; the launch traced here: 26.3 us
  Pallas kernels  25.5 us (97%)
  between operations  0.8 us (3%)
    pallas_call x1, Pallas kernels, on_device(): pl.pallas_call(kernel, out_shape=[pltpu.VMEM(s, bf) for s in shapes], in_...  24.5 us
    pallas_call x1, Pallas kernels, on_device(): pl.pallas_call(write_results, out_shape=[jax.ShapeDtypeStruct(s, bf) for...  0.99 us

profile of v1, /device:TPU:1, one launch (start us, length us, event | category | flops | bytes accessed | tf_op | source)
XLA Modules:
  0.0 26.3 jit_solution(15022827972025499629)
XLA Ops:
  0.6 24.5 %attention_grads.1 = (bf16[64,2048]{1,0:T(8,128)(2,1)S(1)}, bf16[64,256]{1,0:T(8,128)(2,1)S(1)}, bf16[64,256]{1,0:T(8,128)(2,1)S(1)}, bf16[128,2048]{1,0:T(8,128...) custom-call(bf16[64,2048]{1,0:T(8,128)(2,1)} %bitcast.16, bf16[64,256]{1,0:T(8,128)(2,1)} %bitcast.20, ...), custom_call_target="tpu_custom_call" | custom-call | tf_op jit(solution)/shard_map/attention_grads/pallas_call | solution.py:488
  25.1 1.0 %write_results.1 = (bf16[64,2048]{1,0:T(8,128)(2,1)}, bf16[64,256]{1,0:T(8,128)(2,1)}, bf16[64,256]{1,0:T(8,128)(2,1)}, bf16[128,2048]{1,0:T(8,128)(2,1)}, bf16[...) custom-call(bf16[64,2048]{1,0:T(8,128)(2,1)S(1)} %get-tuple-element.18.refs_0_, ...), custom_call_target="tpu_custom_call" | custom-call | tf_op jit(solution)/shard_map/write_results/pallas_call | solution.py:525
